TPU v7x, 32 devices: a whole 2x2x4 slice. The times are simulated.
32 devices in a mesh: groups: 2 (over y), side: 2 (over core), member: 8 (over z, x).
Axes of the slice: x: 2, y: 2, z: 4, core: 2. Of those that a mesh axis runs over, the one named last changes fastest.
Arguments:
- queries: bfloat16 [192, 64, 576], P(('groups', 'side', 'member')), parts along dimension 0, may hold values from -16 to 16
- latent_cache: bfloat16 [192, 128, 576], P(('groups', 'side', 'member')), parts along dimension 0, may hold values from -6 to 6
- lengths: int32 [192], P(('groups', 'side', 'member')), parts along dimension 0, may hold values from 1 to 128, 7680 in all
- moe_input: bfloat16 [192, 3584], P(('groups', 'side', 'member')), parts along dimension 0, may hold values from -6 to 6
- expert_ids: int32 [192, 8], P(('groups', 'side', 'member')), parts along dimension 0, may hold values from 0 to 31, all different within a row; in each aligned block of 6 rows (0 to 5, 6 to 11, ...) at most 2 rows name the same one
- route_scores: float32 [192, 8], P(('groups', 'side', 'member')), parts along dimension 0, may hold values from 0.05 to 1
- placement: int32 [32], replicated, may hold values from 0 to 31, each once
- w_gate: bfloat16 [32, 3584, 2048], P(('side', 'member')), may hold values from -0.09375 to 0.09375
- w_up: bfloat16 [32, 3584, 2048], P(('side', 'member')), may hold values from -0.09375 to 0.09375
- w_down: bfloat16 [32, 2048, 3584], P(('side', 'member')), may hold values from -0.125 to 0.125
Outputs:
- latent_out: bfloat16 [192, 64, 512], P(('groups', 'side', 'member')), parts along dimension 0
- moe_out: bfloat16 [192, 3584], P(('groups', 'side', 'member')), parts along dimension 0
There are 2 independent parts, one for each index of `groups`. A program takes and returns all parts, laid end to end along the dimension named above; an argument that names none is the same for every part. Nothing has to cross between parts.
Inputs may be any that keep to these rules, and one draw needn't show every extreme that they name: `expert_ids`: each row names 8 different experts. Within the rows of one device (aligned blocks of 6 rows) no expert is named by more than 2 rows, a bound that some block reaches. Some request has length exactly 128. The lengths of one part sum to 7680; each part is drawn on its own. `placement`: each slot holds one expert.
All inputs are finite; a program needn't handle non-finite values. No bound on the sum of `lengths` on one device may be relied on, other than what follows from the above.
Results may differ from a plain program's by a relative error of at most 0.0085.
Values may be sent and summed in bfloat16 or wider, within the bound.
A program may use at most 192 MiB of HBM per device.

v0:
```python
import jax
import jax.numpy as jnp
from jax import lax
from jax.sharding import PartitionSpec as P

LATENT = 512
QK_DIM = 192


def attend(queries, latent_cache, lengths):
    score_scale = QK_DIM ** (-0.5)
    scores = (
        jnp.einsum("rhc,rtc->rht", queries, latent_cache, preferred_element_type=jnp.float32)
        * score_scale
    )
    cache_slots = latent_cache.shape[1]
    is_valid = jnp.arange(cache_slots, dtype=jnp.int32)[None, None, :] < lengths[:, None, None]
    scores = jnp.where(is_valid, scores, -jnp.inf)
    row_max = jnp.max(scores, axis=2, keepdims=True)
    exp_scores = jnp.exp(scores - row_max)
    row_total = jnp.sum(exp_scores, axis=2, keepdims=True)
    attn_weights = (exp_scores / row_total).astype(jnp.bfloat16)
    latent_out = jnp.einsum(
        "rht,rtc->rhc",
        attn_weights,
        latent_cache[:, :, :LATENT],
        preferred_element_type=jnp.float32,
    )
    return latent_out.astype(jnp.bfloat16)


def route_plan(expert_ids, route_scores, placement, capacity):
    experts = placement.shape[0]
    slot_table = (placement[:, None] == jnp.arange(experts, dtype=jnp.int32)[None, :]).astype(
        jnp.float32
    )
    picked = (expert_ids[:, :, None] == jnp.arange(experts, dtype=jnp.int32)[None, None, :]).astype(
        jnp.float32
    )
    chosen = jnp.einsum("tke,es->tks", picked, slot_table, precision=lax.Precision.HIGHEST)
    scaled = 2.5 * route_scores / jnp.sum(route_scores, axis=1, keepdims=True)
    taken_slots = jnp.sum(chosen, axis=1)
    slot_weight = jnp.einsum("tk,tks->ts", scaled, chosen, precision=lax.Precision.HIGHEST)
    earlier = jnp.cumsum(taken_slots, axis=0) - taken_slots
    positions = jnp.arange(capacity, dtype=jnp.float32)[None, None, :]
    slot_place = taken_slots[:, :, None] * (earlier[:, :, None] == positions).astype(jnp.float32)
    return (slot_place, slot_weight)


def expert_block(arrived, w_gate, w_up, w_down):
    gate_acts = jnp.einsum("npcd,pdf->npcf", arrived, w_gate, preferred_element_type=jnp.float32)
    up_acts = jnp.einsum("npcd,pdf->npcf", arrived, w_up, preferred_element_type=jnp.float32)
    inner = (jax.nn.silu(gate_acts) * up_acts).astype(jnp.bfloat16)
    return jnp.einsum("npcf,pfd->npcd", inner, w_down, preferred_element_type=jnp.float32).astype(
        jnp.bfloat16
    )


def shards(
    queries,
    latent_cache,
    lengths,
    moe_input,
    expert_ids,
    route_scores,
    placement,
    w_gate,
    w_up,
    w_down,
):
    devices = lax.axis_size(("side", "member"))
    pieces = w_gate.shape[0]
    experts = placement.shape[0]
    split_ways = devices * pieces // experts
    model_width = moe_input.shape[1]
    capacity = moe_input.shape[0] * expert_ids.shape[1] // experts + 1
    slot_place, slot_weight = route_plan(expert_ids, route_scores, placement, capacity)
    place_mask = slot_place.astype(jnp.bfloat16)
    by_slot = jnp.einsum(
        "tsc,td->scd", place_mask, moe_input, preferred_element_type=jnp.float32
    ).astype(jnp.bfloat16)
    outgoing = jnp.repeat(by_slot, split_ways, axis=0).reshape(
        devices, pieces, capacity, model_width
    )
    partial_value = expert_block(
        lax.all_to_all(outgoing, ("side", "member"), split_axis=0, concat_axis=0, tiled=True),
        w_gate,
        w_up,
        w_down,
    )
    returned = lax.all_to_all(
        partial_value, ("side", "member"), split_axis=0, concat_axis=0, tiled=True
    )
    latent_out = attend(queries, latent_cache, lengths)
    returned_slots = returned.reshape(experts, split_ways, capacity, model_width)
    expert_out = jnp.einsum(
        "tsc,sjcd->tsd", place_mask, returned_slots, preferred_element_type=jnp.float32
    )
    moe_sum = jnp.sum(slot_weight[:, :, None] * expert_out, axis=1)
    return (latent_out, moe_sum.astype(jnp.bfloat16))


def solution(mesh):
    return jax.shard_map(
        shards,
        mesh=mesh,
        in_specs=(
            P(("groups", "side", "member"), None, None),
            P(("groups", "side", "member"), None, None),
            P(("groups", "side", "member")),
            P(("groups", "side", "member"), None),
            P(("groups", "side", "member"), None),
            P(("groups", "side", "member"), None),
            P(),
            P(("side", "member"), None, None),
            P(("side", "member"), None, None),
            P(("side", "member"), None, None),
        ),
        out_specs=(
            P(("groups", "side", "member"), None, None),
            P(("groups", "side", "member"), None),
        ),
        check_vma=False,
    )
```

profile of v0, /device:TPU:0, one launch (start us, length us, event | category | flops | bytes accessed | tf_op | source)
XLA Modules:
  0.0 79.3 jit_solution(18083029686872003808)
XLA Ops:
  0.6 0.0 copy-start
  0.6 0.9 %fusion.56 = (f32[6,32]{1,0:T(8,128)S(1)}, f32[6,8,32]{2,1,0:T(8,128)S(1)}) fusion(s32[32]{0:T(128)} %param.16, s32[6,8]{1,0:T(8,128)} %param.14), kind=kOutput, calls=%fused_computation.50 | convolution fusion | flops 102208 | bytes 7232 | tf_op jit(solution)/shard_map/tke,es->tks/dot_general | solution.py:40
  1.6 0.1 copy.21
  1.7 0.1 copy.20
  1.8 1.1 %convolution_convert_fusion = bf16[32,2,3584]{2,0,1:T(8,128)(2,1)S(1)} fusion(bf16[6,3584]{1,0:T(8,128)(2,1)} %param.13, bf16[6,32,2]{0,2,1:T(2,128)(2,1)S(1)} %fusion.44), kind=kOutput, calls=%fused_computation.10 | convolution fusion | flops 2981888 | bytes 502528 | tf_op jit(solution)/shard_map/tsc,td->scd/dot_general | solution.py:79
  2.9 1.2 %copy.32 = bf16[32,2,3584]{2,1,0:T(2,128)(2,1)} copy(bf16[32,2,3584]{2,0,1:T(8,128)(2,1)S(1)} %convolution_convert_fusion) | data formatting | bytes 917504 | tf_op jit(solution)/shard_map/reshape;reshape;broadcast_in_dim | solution.py:82
  4.2 7.4 %all-to-all-start = ((bf16[16,2,2,3584]{3,2,1,0:T(2,128)(2,1)}), bf16[16,2,2,3584]{3,2,1,0:T(2,128)(2,1)S(1)}, u32[]{:S(2)}, u32[]{:S(2)}) async-start(bf16[16,2,2,3584]{3,2,1,0:T(2,128)(2,1)} %bitcast.4), calls=%async_computation | async-start | bytes 917504 | tf_op jit(solution)/shard_map/all_to_all | solution.py:86
  11.5 0.8 %reduce_sum.43 = f32[6]{0:T(128)S(1)} reduce(f32[6,8]{1,0:T(8,128)} %param.15, f32[]{:T(128)} %constant.12.clone.1), dimensions={1}, to_apply=%region_2.0 | reduce | flops 42 | bytes 220 | tf_op jit(solution)/shard_map/reduce_sum | solution.py:41
  12.3 0.8 divide_bitcast_fusion
  13.1 0.2 fusion.51
  13.3 0.1 copy.28
  13.4 12.6 %all-to-all-done = bf16[16,2,2,3584]{3,2,1,0:T(2,128)(2,1)S(1)} async-done(((bf16[16,2,2,3584]{3,2,1,0:T(2,128)(2,1)}), bf16[16,2,2,3584]{3,2,1,0:T(2,128)(2,1)S(1)}, u32[]{:S(2)}, u32[]{:S(2)}) %all-to-all-start) | async-done | bytes 458784 | tf_op jit(solution)/shard_map/all_to_all | solution.py:86
  26.0 12.0 %fusion.14 = f32[16,2,2,2048]{3,0,2,1:T(8,128)S(1)} fusion(bf16[2,3584,2048]{2,1,0:T(8,128)(2,1)} %param.17, bf16[16,2,2,3584]{3,2,1,0:T(2,128)(2,1)S(1)} %all-to-all-done), kind=kOutput, calls=%fused_computation.12 | convolution fusion | flops 939524096 | bytes 30343168 | tf_op jit(solution)/shard_map/npcd,pdf->npcf/dot_general | solution.py:51
  38.0 0.0 copy-start.2
  38.0 0.0 copy-start.1
  38.0 20.8 %fusion.11 = bf16[16,2,2,3584]{3,0,2,1:T(8,128)(2,1)S(1)} fusion(bf16[2,2048,3584]{2,1,0:T(8,128)(2,1)} %param.19, bf16[2,3584,2048]{2,1,0:T(8,128)(2,1)} %param.18, f32[16,2,2,2048]{3,0,2,1:T(8,128)S(1)} %fusion.14, bf16[16,2,2,3584]{3,2,1,0:T(2,128)(2,1)S(1)} %all-to-all-done), kind=kOutput, calls=%fused_computation.11 | convolution fusion | flops 1880064000 | bytes 60162048 | tf_op jit(solution)/shard_map/npcf,pfd->npcd/dot_general | solution.py:54
  58.8 1.2 %copy.26 = bf16[16,2,2,3584]{3,2,1,0:T(2,128)(2,1)} copy(bf16[16,2,2,3584]{3,0,2,1:T(8,128)(2,1)S(1)} %fusion.11) | data formatting | bytes 917504 | tf_op jit(solution)/shard_map/convert_element_type | solution.py:54
  60.1 3.6 %all-to-all-start.1 = ((bf16[16,2,2,3584]{3,2,1,0:T(2,128)(2,1)}), bf16[16,2,2,3584]{3,2,1,0:T(2,128)(2,1)S(1)}, u32[]{:S(2)}, u32[]{:S(2)}) async-start(bf16[16,2,2,3584]{3,2,1,0:T(2,128)(2,1)} %copy.26), calls=%async_computation.1 | async-start | bytes 917504 | tf_op jit(solution)/shard_map/all_to_all | solution.py:91
  63.6 0.0 copy-done.2
  63.6 0.1 iota_compare_fusion.3
  63.7 0.0 copy-done
  63.7 0.0 copy-done.1
  63.7 0.3 fusion.30
  64.0 0.2 fusion.55
  64.2 1.5 %convolution_convert_fusion.1 = bf16[6,64,512]{2,1,0:T(8,128)(2,1)} fusion(bf16[6,128,576]{1,2,0:T(8,128)(2,1)S(1)} %copy-done.1, f32[6,64]{1,0:T(8,128)S(1)} %fusion.55, f32[6,64,128]{2,1,0:T(8,128)S(1)} %fusion.30), kind=kOutput, calls=%fused_computation.17 | convolution fusion | flops 50676224 | bytes 1576960 | tf_op jit(solution)/shard_map/rht,rtc->rhc/dot_general | solution.py:23
  65.8 12.2 %all-to-all-done.1 = bf16[16,2,2,3584]{3,2,1,0:T(2,128)(2,1)S(1)} async-done(((bf16[16,2,2,3584]{3,2,1,0:T(2,128)(2,1)}), bf16[16,2,2,3584]{3,2,1,0:T(2,128)(2,1)S(1)}, u32[]{:S(2)}, u32[]{:S(2)}) %all-to-all-start.1) | async-done | bytes 458784 | tf_op jit(solution)/shard_map/all_to_all | solution.py:91
  78.0 1.3 %fusion.28 = bf16[6,3584]{1,0:T(8,128)(2,1)} fusion(bf16[32,2,3584]{2,1,0:T(2,128)(2,1)S(1)} %bitcast.67, bf16[6,32,2]{0,2,1:T(2,128)(2,1)S(1)} %fusion.44, f32[6,32]{0,1:T(8,128)S(1)} %bitcast.68), kind=kOutput, calls=%fused_computation.16 | convolution fusion | flops 4107264 | bytes 503296 | tf_op jit(solution)/shard_map/tsc,sjcd->tsd/dot_general | solution.py:96
  (3 shorter events, 0.1 us)
Async XLA Ops:
  0.6 63.1 %copy-start = (bf16[6,64,576]{2,1,0:T(8,128)(2,1)S(1)}, bf16[6,64,576]{2,1,0:T(8,128)(2,1)}, u32[]{:S(2)}) copy-start(bf16[6,64,576]{2,1,0:T(8,128)(2,1)} %param.10) | copy-start | bytes 1327108
  4.2 21.8 %all-to-all-start = ((bf16[16,2,2,3584]{3,2,1,0:T(2,128)(2,1)}), bf16[16,2,2,3584]{3,2,1,0:T(2,128)(2,1)S(1)}, u32[]{:S(2)}, u32[]{:S(2)}) async-start(bf16[16,2,2,3584]{3,2,1,0:T(2,128)(2,1)} %bitcast.4), calls=%async_computation | async-start | bytes 917504 | tf_op jit(solution)/shard_map/all_to_all | solution.py:86
  38.0 25.6 %copy-start.2 = (s32[6]{0:T(128)S(1)}, s32[6]{0:T(128)}, u32[]{:S(2)}) copy-start(s32[6]{0:T(128)} %param.12) | copy-start | bytes 76
  38.0 25.7 %copy-start.1 = (bf16[6,128,576]{1,2,0:T(8,128)(2,1)S(1)}, bf16[6,128,576]{1,2,0:T(8,128)(2,1)}, u32[]{:S(2)}) copy-start(bf16[6,128,576]{1,2,0:T(8,128)(2,1)} %param.11) | copy-start | bytes 2654212
  60.1 17.9 %all-to-all-start.1 = ((bf16[16,2,2,3584]{3,2,1,0:T(2,128)(2,1)}), bf16[16,2,2,3584]{3,2,1,0:T(2,128)(2,1)S(1)}, u32[]{:S(2)}, u32[]{:S(2)}) async-start(bf16[16,2,2,3584]{3,2,1,0:T(2,128)(2,1)} %copy.26), calls=%async_computation.1 | async-start | bytes 917504 | tf_op jit(solution)/shard_map/all_to_all | solution.py:91
where the time goes:
time: 79.8 us; the launch traced here: 79.3 us
  matrix products  38.2 us (48%)
  waiting for transfers between devices  24.8 us (31%)
  starting transfers between devices  10.9 us (14%)
  local copies, waits for them, and re-layouts  2.78 us (3%)
  other arithmetic  1.89 us (2%)
    dot_general x1, matrix products, expert_block(): jnp.einsum('npcf,pfd->npcd', inner, w_down, preferred_element_type=jnp.fl...  20.8 us
    all_to_all x1, waiting for transfers between devices, shards(): lax.all_to_all(outgoing, ('side', 'member'), split_axis=0, concat_axis=0,...  12.6 us
    all_to_all x1, waiting for transfers between devices, shards(): lax.all_to_all(partial_value, ('side', 'member'), split_axis=0, concat_ax...  12.2 us
    dot_general x1, matrix products, expert_block(): jnp.einsum('npcd,pdf->npcf', arrived, w_gate, preferred_element_type=jnp....  12 us
    all_to_all x1, starting transfers between devices, shards(): lax.all_to_all(outgoing, ('side', 'member'), split_axis=0, concat_axis=0,...  7.36 us
    all_to_all x1, starting transfers between devices, shards(): lax.all_to_all(partial_value, ('side', 'member'), split_axis=0, concat_ax...  3.56 us
  transfers between devices with their start and end apart: 2, of which 2 were waited for; matrix products, arithmetic and copies ran while one was open for 5% of the time, Pallas kernels for 0%

commit v1 on v0

v1 whole, which is shorter than its diff:
```python
import functools

import jax
import jax.numpy as jnp
from jax import lax
from jax.experimental import pallas as pl
from jax.experimental.pallas import tpu as pltpu
from jax.sharding import PartitionSpec as P

LATENT = 512
QK_DIM = 192
CHUNK = 512
MESH = pl.DeviceIdType.MESH


def row_tables(placement_ref, ids, scores, n, pieces, cap, experts, rows):
    split = n * pieces // experts
    tokens, routed = ids.shape
    lanes = lax.broadcasted_iota(jnp.int32, (8, rows), 1).astype(jnp.float32)
    block = jnp.floor((lanes + 0.5) * (1.0 / cap))
    position = lanes - cap * block
    piece = jnp.floor((block + 0.5) * (1.0 / n))
    device = block - n * piece
    slot = jnp.floor((device * pieces + piece + 0.5) * (1.0 / split)).astype(jnp.int32)
    expert = jnp.full((8, rows), -1, jnp.int32)
    for e in range(experts):
        expert = jnp.where(slot == placement_ref[e], e, expert)
    expert, position = expert[:tokens], position[:tokens]
    mix = 2.5 * scores / jnp.sum(scores, axis=1, keepdims=True)
    hits = jnp.zeros((tokens, rows), jnp.float32)
    weight = jnp.zeros((tokens, rows), jnp.float32)
    for k in range(routed):
        same = ids[:, k : k + 1] == expert
        hits = jnp.where(same, 1.0, hits)
        weight = jnp.where(same, mix[:, k : k + 1], weight)
    token = lax.broadcasted_iota(jnp.int32, (tokens, rows), 0)
    earlier = jnp.zeros((tokens, rows), jnp.float32)
    for t in range(tokens - 1):
        earlier = earlier + jnp.where(token > t, hits[t : t + 1], 0.0)
    place = jnp.where(earlier == position, hits, 0.0)
    return place, place * weight


def kernel(
    n, n_member, pieces, cap, experts,
    placement_ref, lengths_ref, ids_ref, scores_ref, x_ref,
    q_hbm, c_hbm, wg_hbm, wu_hbm, wd_hbm,
    latent_hbm, moe_ref,
    q_ref, c_ref, o_ref, wg_ref, wu_ref, wd_ref,
    xs_ref, send_ref, arr_ref, x2_ref, ag_ref, au_ref, inner_ref, yb_ref, ret_ref, mixw_ref, out_ref,
    q_sem, c_sem, o_sem, wg_sem, wu_sem, wd_sem,
    dsend_sem, drecv_sem, rsend_sem, rrecv_sem,
):
    side, member = lax.axis_index("side"), lax.axis_index("member")
    me = side * n_member + member
    tokens, width = x_ref.shape
    hidden = wg_hbm.shape[2]
    requests = q_hbm.shape[0]
    rows = pieces * n * cap
    per = n * cap
    nk = width // CHUNK

    def peer(i):
        d = lax.rem(me + i, n)
        return d, {"side": d // n_member, "member": lax.rem(d, n_member)}

    def gate_copy(p, i):
        return pltpu.make_async_copy(
            wg_hbm.at[p, pl.ds(pl.multiple_of(i * CHUNK, CHUNK), CHUNK)], wg_ref.at[i], wg_sem.at[i]
        )

    def up_copy(p, i):
        return pltpu.make_async_copy(
            wu_hbm.at[p, pl.ds(pl.multiple_of(i * CHUNK, CHUNK), CHUNK)], wu_ref.at[i], wu_sem.at[i]
        )

    def down_copy(p, i):
        return pltpu.make_async_copy(
            wd_hbm.at[p, :, pl.ds(pl.multiple_of(i * CHUNK, CHUNK), CHUNK)], wd_ref.at[i], wd_sem.at[i]
        )

    barrier = pltpu.get_barrier_semaphore()

    @pl.loop(1, n)
    def _(i):
        pl.semaphore_signal(barrier, inc=1, device_id=peer(i)[1], device_id_type=MESH)

    q_copy = pltpu.make_async_copy(q_hbm, q_ref, q_sem)
    c_copy = pltpu.make_async_copy(c_hbm, c_ref, c_sem)
    o_copy = pltpu.make_async_copy(o_ref, latent_hbm, o_sem)
    q_copy.start()
    c_copy.start()

    @pl.loop(0, nk)
    def _(i):
        gate_copy(0, i).start()
        up_copy(0, i).start()

    @pl.loop(0, nk)
    def _(i):
        down_copy(0, i).start()

    lanes = -(-rows // 128) * 128
    place, mixw = row_tables(
        placement_ref, ids_ref[...], scores_ref[...], n, pieces, cap, experts, lanes
    )
    high = mixw.astype(jnp.bfloat16)
    rest = mixw - high.astype(jnp.float32)
    mid = rest.astype(jnp.bfloat16)
    low = (rest - mid.astype(jnp.float32)).astype(jnp.bfloat16)
    pad = jnp.zeros((8 - tokens, lanes), jnp.float32)
    mixw_ref[...] = jnp.concatenate(
        [
            jnp.concatenate([v.astype(jnp.float32), pad], axis=0)
            for v in (high, mid, low, jnp.zeros_like(low))
        ],
        axis=0,
    ).astype(jnp.bfloat16)
    picks = jnp.concatenate([place, jnp.zeros((16 - tokens, lanes), jnp.float32)], axis=0)
    picks = picks.T.astype(jnp.bfloat16)
    xs_ref[...] = jnp.zeros_like(xs_ref)
    xs_ref[0:tokens, :] = x_ref[...]
    for p in range(pieces):
        for j in range(nk):
            cols = pl.ds(j * CHUNK, CHUNK)
            made = jnp.dot(
                picks[p * per : (p + 1) * per], xs_ref[:, cols], preferred_element_type=jnp.float32
            )
            send_ref[p, :, :, cols] = made.reshape(n, cap, CHUNK).astype(jnp.bfloat16)

    pl.semaphore_wait(barrier, n - 1)
    for p in range(pieces):

        @pl.loop(1, n)
        def _(i, p=p):
            d, where = peer(i)
            pltpu.make_async_remote_copy(
                src_ref=send_ref.at[p, d],
                dst_ref=arr_ref.at[p, me],
                send_sem=dsend_sem.at[p],
                recv_sem=drecv_sem.at[p],
                device_id=where,
                device_id_type=MESH,
            ).start()

        arr_ref[p, me] = send_ref[p, me]

    q_copy.wait()
    c_copy.wait()
    scale = QK_DIM ** (-0.5)
    for r in range(requests):
        s = lax.dot_general(
            q_ref[r], c_ref[r], (((1,), (1,)), ((), ())), preferred_element_type=jnp.float32
        ) * scale
        valid = lax.broadcasted_iota(jnp.int32, s.shape, 1) < lengths_ref[r]
        s = jnp.where(valid, s, -jnp.inf)
        e = jnp.exp(s - jnp.max(s, axis=1, keepdims=True))
        a = (e / jnp.sum(e, axis=1, keepdims=True)).astype(jnp.bfloat16)
        o_ref[r] = jnp.dot(
            a, c_ref[r, :, :LATENT], preferred_element_type=jnp.float32
        ).astype(jnp.bfloat16)
    o_copy.start()

    def all_but_one(ref):
        return ref.at[pl.ds(0, n - 1)]

    def drain(ref, sem):
        view = all_but_one(ref)
        pltpu.make_async_copy(view, view, sem).wait()

    def combine(p, j):
        drain(ret_ref.at[p, j], rrecv_sem.at[p, j])
        got = ret_ref[p, j].astype(jnp.float32).reshape(per, CHUNK).astype(jnp.bfloat16)
        part = jnp.dot(
            mixw_ref[:, p * per : (p + 1) * per], got, preferred_element_type=jnp.float32
        )
        part = part[0:8] + part[8:16] + part[16:24]
        return part

    for p in range(pieces):
        drain(arr_ref.at[p], drecv_sem.at[p])
        for j in range(nk):
            cols = pl.ds(j * CHUNK, CHUNK)
            x2_ref[:, cols] = (
                arr_ref[p, :, :, cols].astype(jnp.float32).reshape(per, CHUNK).astype(jnp.bfloat16)
            )
        ag_ref[...] = jnp.zeros_like(ag_ref)
        au_ref[...] = jnp.zeros_like(au_ref)

        @pl.loop(0, nk)
        def _(i, p=p):
            xk = x2_ref[:, pl.ds(pl.multiple_of(i * CHUNK, CHUNK), CHUNK)]
            gate_copy(p, i).wait()
            ag_ref[...] += jnp.dot(xk, wg_ref[i], preferred_element_type=jnp.float32)
            if p + 1 < pieces:
                gate_copy(p + 1, i).start()
            up_copy(p, i).wait()
            au_ref[...] += jnp.dot(xk, wu_ref[i], preferred_element_type=jnp.float32)
            if p + 1 < pieces:
                up_copy(p + 1, i).start()

        g = ag_ref[...]
        inner_ref[...] = (g / (1.0 + jnp.exp(-g)) * au_ref[...]).astype(jnp.bfloat16)
        if p > 0:
            for j in range(nk):
                cols = pl.ds(j * CHUNK, CHUNK)
                before = 0.0 if p == 1 else out_ref[:, cols]
                out_ref[:, cols] = before + combine(p - 1, j)

        @pl.loop(0, nk)
        def _(j, p=p):
            down_copy(p, j).wait()
            y = jnp.dot(inner_ref[...], wd_ref[j], preferred_element_type=jnp.float32)
            if p + 1 < pieces:
                down_copy(p + 1, j).start()
            yb_ref[p, j] = y.reshape(n, cap, CHUNK).astype(jnp.bfloat16)

            @pl.loop(1, n)
            def _(i):
                d, where = peer(i)
                pltpu.make_async_remote_copy(
                    src_ref=yb_ref.at[p, j, d],
                    dst_ref=ret_ref.at[p, j, me],
                    send_sem=rsend_sem.at[p, j],
                    recv_sem=rrecv_sem.at[p, j],
                    device_id=where,
                    device_id_type=MESH,
                ).start()

            ret_ref[p, j, me] = yb_ref[p, j, me]

    last = pieces - 1
    for j in range(nk):
        cols = pl.ds(j * CHUNK, CHUNK)
        total = combine(last, j)
        if pieces > 1:
            total = total + out_ref[:, cols]
        moe_ref[:, cols] = total[0:tokens].astype(jnp.bfloat16)

    o_copy.wait()
    for p in range(pieces):
        drain(send_ref.at[p], dsend_sem.at[p])

        @pl.loop(0, nk)
        def _(j, p=p):
            drain(yb_ref.at[p, j], rsend_sem.at[p, j])


def shards(
    queries,
    latent_cache,
    lengths,
    moe_input,
    expert_ids,
    route_scores,
    placement,
    w_gate,
    w_up,
    w_down,
):
    n_side, n_member = lax.axis_size("side"), lax.axis_size("member")
    n = n_side * n_member
    pieces, width, hidden = w_gate.shape
    experts = placement.shape[0]
    tokens = moe_input.shape[0]
    cap = tokens * expert_ids.shape[1] // experts + 1
    per = n * cap
    rows = pieces * per
    lanes = -(-rows // 128) * 128
    nk = width // CHUNK
    requests, heads, entry = queries.shape
    bf16, f32 = jnp.bfloat16, jnp.float32
    vmem = pl.BlockSpec(memory_space=pltpu.VMEM)
    smem = pl.BlockSpec(memory_space=pltpu.SMEM)
    hbm = pl.BlockSpec(memory_space=pl.ANY)
    dma = pltpu.SemaphoreType.DMA
    latent_out, moe_out = pl.pallas_call(
        functools.partial(kernel, n, n_member, pieces, cap, experts),
        out_shape=(
            jax.ShapeDtypeStruct((requests, heads, LATENT), bf16),
            jax.ShapeDtypeStruct((tokens, width), bf16),
        ),
        in_specs=[smem, smem, vmem, vmem, vmem, hbm, hbm, hbm, hbm, hbm],
        out_specs=(hbm, vmem),
        scratch_shapes=[
            pltpu.VMEM(queries.shape, bf16),
            pltpu.VMEM(latent_cache.shape, bf16),
            pltpu.VMEM((requests, heads, LATENT), bf16),
            pltpu.VMEM((nk, CHUNK, hidden), bf16),
            pltpu.VMEM((nk, CHUNK, hidden), bf16),
            pltpu.VMEM((nk, hidden, CHUNK), bf16),
            pltpu.VMEM((16, width), bf16),
            pltpu.VMEM((pieces, n, cap, width), bf16),
            pltpu.VMEM((pieces, n, cap, width), bf16),
            pltpu.VMEM((per, width), bf16),
            pltpu.VMEM((per, hidden), f32),
            pltpu.VMEM((per, hidden), f32),
            pltpu.VMEM((per, hidden), bf16),
            pltpu.VMEM((pieces, nk, n, cap, CHUNK), bf16),
            pltpu.VMEM((pieces, nk, n, cap, CHUNK), bf16),
            pltpu.VMEM((32, lanes), bf16),
            pltpu.VMEM((8, width), f32),
            dma,
            dma,
            dma,
            dma((nk,)),
            dma((nk,)),
            dma((nk,)),
            dma((pieces,)),
            dma((pieces,)),
            dma((pieces, nk)),
            dma((pieces, nk)),
        ],
        compiler_params=pltpu.CompilerParams(
            collective_id=0, has_side_effects=True, vmem_limit_bytes=60 * 1024 * 1024
        ),
        cost_estimate=pl.CostEstimate(
            flops=6 * rows * width * hidden,
            bytes_accessed=6 * pieces * width * hidden,
            transcendentals=per * hidden,
        ),
    )(
        placement,
        lengths,
        expert_ids,
        route_scores,
        moe_input,
        queries,
        latent_cache,
        w_gate,
        w_up,
        w_down,
    )
    return (latent_out, moe_out)


def solution(mesh):
    return jax.shard_map(
        shards,
        mesh=mesh,
        in_specs=(
            P(("groups", "side", "member"), None, None),
            P(("groups", "side", "member"), None, None),
            P(("groups", "side", "member")),
            P(("groups", "side", "member"), None),
            P(("groups", "side", "member"), None),
            P(("groups", "side", "member"), None),
            P(),
            P(("side", "member"), None, None),
            P(("side", "member"), None, None),
            P(("side", "member"), None, None),
        ),
        out_specs=(
            P(("groups", "side", "member"), None, None),
            P(("groups", "side", "member"), None),
        ),
        check_vma=False,
    )
```

time: 79.8 us -> 53.3 us (0.67)
  Pallas kernels: 0 us -> 47 us
  matrix products: 38.2 us -> 0 us
  waiting for transfers between devices: 24.8 us -> 0 us
  starting transfers between devices: 10.9 us -> 0 us
  local copies, waits for them, and re-layouts: 2.78 us -> 5.45 us
  other arithmetic: 1.89 us -> 0 us
    pallas_call x0 -> x1, Pallas kernels: none -> 47 us  [shards(): pl.pallas_call(functools.partial(kernel, n, n_member, pieces, cap, expert...]
    dot_general x8 -> x0, matrix products: 38.2 us -> none  [the longest x1 20.8 us: expert_block(): jnp.einsum('npcf,pfd->npcd', inner, w_down, preferred_element_type=jnp.fl...]
    all_to_all x2 -> x0, waiting for transfers between devices: 24.8 us -> none  [the longest x1 12.6 us: shards(): lax.all_to_all(outgoing, ('side', 'member'), split_axis=0, concat_axis=0,...]
    all_to_all x2 -> x0, starting transfers between devices: 10.9 us -> none  [the longest x1 7.36 us: shards(): lax.all_to_all(outgoing, ('side', 'member'), split_axis=0, concat_axis=0,...]
    unnamed x6 -> x3, local copies, waits for them, and re-layouts: 0.02 us -> 5.45 us
    another operation x1 -> x0, local copies, waits for them, and re-layouts: 1.24 us -> none  [shards(): jnp.repeat(by_slot, split_ways, axis=0)]
    convert_element_type x1 -> x0, local copies, waits for them, and re-layouts: 1.24 us -> none  [expert_block(): jnp.einsum('npcf,pfd->npcd', inner, w_down, preferred_element_type=jnp.fl...]
    reduce_sum x1 -> x0, other arithmetic: 0.81 us -> none  [route_plan(): scaled = 2.5 * route_scores / jnp.sum(route_scores, axis=1, keepdims=True)]
  transfers between devices with their start and end apart: 2 -> 0, of which waited for: 2 -> 0; matrix products, arithmetic and copies ran while one was open for 5% -> 0% of each run, Pallas kernels for 0% -> 0%
where the time goes in v1:
time: 53.3 us; the launch traced here: 53.1 us
  Pallas kernels  47 us (88%)
  local copies, waits for them, and re-layouts  5.45 us (10%)
  between operations  0.64 us (1%)
    pallas_call x1, Pallas kernels, shards(): pl.pallas_call(functools.partial(kernel, n, n_member, pieces, cap, expert...  47 us
    unnamed x3, local copies, waits for them, and re-layouts  5.45 us

profile of v1, /device:TPU:0, one launch (start us, length us, event | category | flops | bytes accessed | tf_op | source)
XLA Modules:
  0.0 53.1 jit_solution(1654049372359450548)
XLA Ops:
  0.6 2.2 %copy.12.c_hbm = bf16[6,128,576]{2,1,0:T(8,128)(2,1)} copy(bf16[6,128,576]{1,2,0:T(8,128)(2,1)} %param.11) | data formatting | bytes 1769472 | tf_op args[1]
  2.9 47.0 %shard_map.113 = (bf16[6,64,512]{2,1,0:T(8,128)(2,1)}, bf16[6,3584]{1,0:T(8,128)(2,1)}) custom-call(s32[32]{0:T(128)} %placement_ref.1, s32[6]{0:T(128)} %lengths_ref.1, s32[6,8]{1,0:T(8,128)} %ids_ref.1, f32[6,8]{1,0:T(8,128)} %scores_ref.1, bf16[6,3584]{1,0:T(8,128)(2,1)} %x_ref.1, bf16[6,64,576]{2,1,0:T(8,128)(2,1)} %q_hbm.1, ...), custom_call_target="tpu_custom_call" | custom-call | flops 2818572288 | bytes 88080384 | tf_op jit(solution)/shard_map/pallas_call | solution.py:277
  49.8 1.8 %copy.15 = bf16[6,64,512]{2,1,0:T(8,128)(2,1)} copy(bf16[6,64,512]{2,1,0:T(8,128)(2,1)} %get-tuple-element.4) | data formatting | bytes 786432
  51.6 1.4 %copy.16 = bf16[6,3584]{1,0:T(8,128)(2,1)} copy(bf16[6,3584]{1,0:T(8,128)(2,1)} %get-tuple-element.5) | data formatting | bytes 86016

commit v2 on v1

--- a/solution.py
+++ b/solution.py
@@ -60,9 +60,14 @@
     per = n * cap
     nk = width // CHUNK
 
-    def peer(i):
-        d = lax.rem(me + i, n)
-        return d, {"side": d // n_member, "member": lax.rem(d, n_member)}
+    def each_peer(visit):
+        for step in range(n // n_member):
+            there = lax.rem(side + step, n // n_member)
+
+            @pl.loop(1 if step == 0 else 0, n_member)
+            def _(i):
+                other = lax.rem(member + i, n_member)
+                visit(there * n_member + other, {"side": there, "member": other})
 
     def gate_copy(p, i):
         return pltpu.make_async_copy(
@@ -81,9 +86,11 @@
 
     barrier = pltpu.get_barrier_semaphore()
 
-    @pl.loop(1, n)
-    def _(i):
-        pl.semaphore_signal(barrier, inc=1, device_id=peer(i)[1], device_id_type=MESH)
+    each_peer(
+        lambda d, where: pl.semaphore_signal(
+            barrier, inc=1, device_id=where, device_id_type=MESH
+        )
+    )
 
     q_copy = pltpu.make_async_copy(q_hbm, q_ref, q_sem)
     c_copy = pltpu.make_async_copy(c_hbm, c_ref, c_sem)
@@ -131,9 +138,7 @@
     pl.semaphore_wait(barrier, n - 1)
     for p in range(pieces):
 
-        @pl.loop(1, n)
-        def _(i, p=p):
-            d, where = peer(i)
+        def send_slots(d, where, p=p):
             pltpu.make_async_remote_copy(
                 src_ref=send_ref.at[p, d],
                 dst_ref=arr_ref.at[p, me],
@@ -143,6 +148,7 @@
                 device_id_type=MESH,
             ).start()
 
+        each_peer(send_slots)
         arr_ref[p, me] = send_ref[p, me]
 
     q_copy.wait()
@@ -150,32 +156,34 @@
     scale = QK_DIM ** (-0.5)
     for r in range(requests):
         s = lax.dot_general(
-            q_ref[r], c_ref[r], (((1,), (1,)), ((), ())), preferred_element_type=jnp.float32
+            q_ref[r], c_ref[r], (((1,), (0,)), ((), ())), preferred_element_type=jnp.float32
         ) * scale
         valid = lax.broadcasted_iota(jnp.int32, s.shape, 1) < lengths_ref[r]
         s = jnp.where(valid, s, -jnp.inf)
         e = jnp.exp(s - jnp.max(s, axis=1, keepdims=True))
         a = (e / jnp.sum(e, axis=1, keepdims=True)).astype(jnp.bfloat16)
-        o_ref[r] = jnp.dot(
-            a, c_ref[r, :, :LATENT], preferred_element_type=jnp.float32
+        o_ref[r] = lax.dot_general(
+            a, c_ref[r, :LATENT], (((1,), (1,)), ((), ())), preferred_element_type=jnp.float32
         ).astype(jnp.bfloat16)
     o_copy.start()
 
-    def all_but_one(ref):
-        return ref.at[pl.ds(0, n - 1)]
-
     def drain(ref, sem):
-        view = all_but_one(ref)
+        view = ref.at[pl.ds(0, n - 1)]
         pltpu.make_async_copy(view, view, sem).wait()
 
+    cut = nk * 4 // 7
+    groups = [[(0, nk)]] * (pieces - 1) + [[(0, cut), (cut, nk)]]
+
+    def columns(group):
+        return pl.ds(group[0] * CHUNK, (group[1] - group[0]) * CHUNK)
+
     def combine(p, j):
-        drain(ret_ref.at[p, j], rrecv_sem.at[p, j])
-        got = ret_ref[p, j].astype(jnp.float32).reshape(per, CHUNK).astype(jnp.bfloat16)
+        got = ret_ref[p, :, :, pl.ds(j * CHUNK, CHUNK)]
+        got = got.astype(jnp.float32).reshape(per, CHUNK).astype(jnp.bfloat16)
         part = jnp.dot(
             mixw_ref[:, p * per : (p + 1) * per], got, preferred_element_type=jnp.float32
         )
-        part = part[0:8] + part[8:16] + part[16:24]
-        return part
+        return part[0:8] + part[8:16] + part[16:24]
 
     for p in range(pieces):
         drain(arr_ref.at[p], drecv_sem.at[p])
@@ -202,48 +210,56 @@
         g = ag_ref[...]
         inner_ref[...] = (g / (1.0 + jnp.exp(-g)) * au_ref[...]).astype(jnp.bfloat16)
         if p > 0:
+            drain(ret_ref.at[p - 1], rrecv_sem.at[p - 1, 0])
             for j in range(nk):
                 cols = pl.ds(j * CHUNK, CHUNK)
                 before = 0.0 if p == 1 else out_ref[:, cols]
                 out_ref[:, cols] = before + combine(p - 1, j)
 
-        @pl.loop(0, nk)
-        def _(j, p=p):
-            down_copy(p, j).wait()
-            y = jnp.dot(inner_ref[...], wd_ref[j], preferred_element_type=jnp.float32)
-            if p + 1 < pieces:
-                down_copy(p + 1, j).start()
-            yb_ref[p, j] = y.reshape(n, cap, CHUNK).astype(jnp.bfloat16)
-
-            @pl.loop(1, n)
-            def _(i):
-                d, where = peer(i)
+        for g, group in enumerate(groups[p]):
+            for j in range(*group):
+                down_copy(p, j).wait()
+                y = jnp.dot(inner_ref[...], wd_ref[j], preferred_element_type=jnp.float32)
+                if p + 1 < pieces:
+                    down_copy(p + 1, j).start()
+                yb_ref[p, :, :, pl.ds(j * CHUNK, CHUNK)] = y.reshape(n, cap, CHUNK).astype(
+                    jnp.bfloat16
+                )
+            cols = columns(group)
+
+            def send_back(d, where, p=p, g=g, cols=cols):
                 pltpu.make_async_remote_copy(
-                    src_ref=yb_ref.at[p, j, d],
-                    dst_ref=ret_ref.at[p, j, me],
-                    send_sem=rsend_sem.at[p, j],
-                    recv_sem=rrecv_sem.at[p, j],
+                    src_ref=yb_ref.at[p, d, :, cols],
+                    dst_ref=ret_ref.at[p, me, :, cols],
+                    send_sem=rsend_sem.at[p, g],
+                    recv_sem=rrecv_sem.at[p, g],
                     device_id=where,
                     device_id_type=MESH,
                 ).start()
 
-            ret_ref[p, j, me] = yb_ref[p, j, me]
+            each_peer(send_back)
+            ret_ref[p, me, :, cols] = yb_ref[p, me, :, cols]
 
     last = pieces - 1
-    for j in range(nk):
-        cols = pl.ds(j * CHUNK, CHUNK)
-        total = combine(last, j)
-        if pieces > 1:
-            total = total + out_ref[:, cols]
-        moe_ref[:, cols] = total[0:tokens].astype(jnp.bfloat16)
+    for g, group in enumerate(groups[last]):
+        drain(ret_ref.at[last, :, :, columns(group)], rrecv_sem.at[last, g])
+        for j in range(*group):
+            cols = pl.ds(j * CHUNK, CHUNK)
+            total = combine(last, j)
+            if pieces > 1:
+                total = total + out_ref[:, cols]
+            moe_ref[:, cols] = total[0:tokens].astype(jnp.bfloat16)
 
     o_copy.wait()
     for p in range(pieces):
         drain(send_ref.at[p], dsend_sem.at[p])
-
-        @pl.loop(0, nk)
-        def _(j, p=p):
-            drain(yb_ref.at[p, j], rsend_sem.at[p, j])
+        for g, group in enumerate(groups[p]):
+            drain(yb_ref.at[p, :, :, columns(group)], rsend_sem.at[p, g])
+
+
+def hand_over(latent_ref, moe_ref, latent_out_ref, moe_out_ref):
+    latent_out_ref[...] = latent_ref[...]
+    moe_out_ref[...] = moe_ref[...]
 
 
 def shards(
@@ -269,6 +285,7 @@
     lanes = -(-rows // 128) * 128
     nk = width // CHUNK
     requests, heads, entry = queries.shape
+    cache_columns = jnp.swapaxes(latent_cache, 1, 2)
     bf16, f32 = jnp.bfloat16, jnp.float32
     vmem = pl.BlockSpec(memory_space=pltpu.VMEM)
     smem = pl.BlockSpec(memory_space=pltpu.SMEM)
@@ -284,7 +301,7 @@
         out_specs=(hbm, vmem),
         scratch_shapes=[
             pltpu.VMEM(queries.shape, bf16),
-            pltpu.VMEM(latent_cache.shape, bf16),
+            pltpu.VMEM(cache_columns.shape, bf16),
             pltpu.VMEM((requests, heads, LATENT), bf16),
             pltpu.VMEM((nk, CHUNK, hidden), bf16),
             pltpu.VMEM((nk, CHUNK, hidden), bf16),
@@ -296,8 +313,8 @@
             pltpu.VMEM((per, hidden), f32),
             pltpu.VMEM((per, hidden), f32),
             pltpu.VMEM((per, hidden), bf16),
-            pltpu.VMEM((pieces, nk, n, cap, CHUNK), bf16),
-            pltpu.VMEM((pieces, nk, n, cap, CHUNK), bf16),
+            pltpu.VMEM((pieces, n, cap, width), bf16),
+            pltpu.VMEM((pieces, n, cap, width), bf16),
             pltpu.VMEM((32, lanes), bf16),
             pltpu.VMEM((8, width), f32),
             dma,
@@ -308,8 +325,8 @@
             dma((nk,)),
             dma((pieces,)),
             dma((pieces,)),
-            dma((pieces, nk)),
-            dma((pieces, nk)),
+            dma((pieces, 2)),
+            dma((pieces, 2)),
         ],
         compiler_params=pltpu.CompilerParams(
             collective_id=0, has_side_effects=True, vmem_limit_bytes=60 * 1024 * 1024
@@ -326,12 +343,20 @@
         route_scores,
         moe_input,
         queries,
-        latent_cache,
+        cache_columns,
         w_gate,
         w_up,
         w_down,
     )
-    return (latent_out, moe_out)
+    return pl.pallas_call(
+        hand_over,
+        out_shape=(
+            jax.ShapeDtypeStruct(latent_out.shape, bf16),
+            jax.ShapeDtypeStruct(moe_out.shape, bf16),
+        ),
+        in_specs=[vmem, vmem],
+        out_specs=(vmem, vmem),
+    )(latent_out, moe_out)
 
 
 def solution(mesh):

time: 53.3 us -> 45.1 us (0.85)
  local copies, waits for them, and re-layouts: 5.45 us -> 0 us
  Pallas kernels: 47 us -> 44.3 us
    unnamed x3 -> x0, local copies, waits for them, and re-layouts: 5.45 us -> none
    pallas_call x1, Pallas kernels: 47 us -> 42.5 us  [shards(): pl.pallas_call(functools.partial(kernel, n, n_member, pieces, cap, expert...]
    pallas_call x0 -> x1, Pallas kernels: none -> 1.78 us  [shards(): pl.pallas_call(hand_over, out_shape=(jax.ShapeDtypeStruct(latent_out.shap...]
where the time goes in v2:
time: 45.1 us; the launch traced here: 44.9 us
  Pallas kernels  44.3 us (98%)
  between operations  0.64 us (1%)
    pallas_call x1, Pallas kernels, shards(): pl.pallas_call(functools.partial(kernel, n, n_member, pieces, cap, expert...  42.5 us
    pallas_call x1, Pallas kernels, shards(): pl.pallas_call(hand_over, out_shape=(jax.ShapeDtypeStruct(latent_out.shap...  1.78 us

profile of v2, /device:TPU:0, one launch (start us, length us, event | category | flops | bytes accessed | tf_op | source)
XLA Modules:
  0.0 44.9 jit_solution(17096665747160673877)
XLA Ops:
  0.6 42.5 %shard_map.113 = (bf16[6,64,512]{2,1,0:T(8,128)(2,1)}, bf16[6,3584]{1,0:T(8,128)(2,1)}) custom-call(s32[32]{0:T(128)} %placement_ref.1, s32[6]{0:T(128)} %lengths_ref.1, s32[6,8]{1,0:T(8,128)} %ids_ref.1, f32[6,8]{1,0:T(8,128)} %scores_ref.1, bf16[6,3584]{1,0:T(8,128)(2,1)} %x_ref.1, bf16[6,64,576]{2,1,0:T(8,128)(2,1)} %q_hbm.1, ...), custom_call_target="tpu_custom_call" | custom-call | flops 2818572288 | bytes 88080384 | tf_op jit(solution)/shard_map/pallas_call | solution.py:294
  43.1 1.8 %shard_map.114 = (bf16[6,64,512]{2,1,0:T(8,128)(2,1)}, bf16[6,3584]{1,0:T(8,128)(2,1)}) custom-call(bf16[6,64,512]{2,1,0:T(8,128)(2,1)} %get-tuple-element.4.latent_ref, bf16[6,3584]{1,0:T(8,128)(2,1)} %get-tuple-element.5.moe_ref), custom_call_target="tpu_custom_call" | custom-call | tf_op jit(solution)/shard_map/pallas_call | solution.py:351

commit v3 on v2

--- a/solution.py
+++ b/solution.py
@@ -11,7 +11,6 @@
 QK_DIM = 192
 CHUNK = 512
 MESH = pl.DeviceIdType.MESH
-
 
 def row_tables(placement_ref, ids, scores, n, pieces, cap, experts, rows):
     split = n * pieces // experts
@@ -39,7 +38,6 @@
         earlier = earlier + jnp.where(token > t, hits[t : t + 1], 0.0)
     place = jnp.where(earlier == position, hits, 0.0)
     return place, place * weight
-
 
 def kernel(
     n, n_member, pieces, cap, experts,
@@ -135,20 +133,30 @@
             )
             send_ref[p, :, :, cols] = made.reshape(n, cap, CHUNK).astype(jnp.bfloat16)
 
+    cut, far = nk * 2 // 7, nk * 4 // 7
+
+    out_groups = [[(0, cut), (cut, far), (far, nk)]] + [[(0, nk)]] * (pieces - 1)
+    groups = [[(0, nk)]] * (pieces - 1) + [[(0, far), (far, nk)]]
+
+    def columns(group):
+        return pl.ds(group[0] * CHUNK, (group[1] - group[0]) * CHUNK)
+
     pl.semaphore_wait(barrier, n - 1)
     for p in range(pieces):
-
-        def send_slots(d, where, p=p):
-            pltpu.make_async_remote_copy(
-                src_ref=send_ref.at[p, d],
-                dst_ref=arr_ref.at[p, me],
-                send_sem=dsend_sem.at[p],
-                recv_sem=drecv_sem.at[p],
-                device_id=where,
-                device_id_type=MESH,
-            ).start()
-
-        each_peer(send_slots)
+        for g, group in enumerate(out_groups[p]):
+            cols = columns(group)
+
+            def send_slots(d, where, p=p, g=g, cols=cols):
+                pltpu.make_async_remote_copy(
+                    src_ref=send_ref.at[p, d, :, cols],
+                    dst_ref=arr_ref.at[p, me, :, cols],
+                    send_sem=dsend_sem.at[p, g],
+                    recv_sem=drecv_sem.at[p, g],
+                    device_id=where,
+                    device_id_type=MESH,
+                ).start()
+
+            each_peer(send_slots)
         arr_ref[p, me] = send_ref[p, me]
 
     q_copy.wait()
@@ -171,12 +179,6 @@
         view = ref.at[pl.ds(0, n - 1)]
         pltpu.make_async_copy(view, view, sem).wait()
 
-    cut = nk * 4 // 7
-    groups = [[(0, nk)]] * (pieces - 1) + [[(0, cut), (cut, nk)]]
-
-    def columns(group):
-        return pl.ds(group[0] * CHUNK, (group[1] - group[0]) * CHUNK)
-
     def combine(p, j):
         got = ret_ref[p, :, :, pl.ds(j * CHUNK, CHUNK)]
         got = got.astype(jnp.float32).reshape(per, CHUNK).astype(jnp.bfloat16)
@@ -186,26 +188,27 @@
         return part[0:8] + part[8:16] + part[16:24]
 
     for p in range(pieces):
-        drain(arr_ref.at[p], drecv_sem.at[p])
-        for j in range(nk):
-            cols = pl.ds(j * CHUNK, CHUNK)
-            x2_ref[:, cols] = (
-                arr_ref[p, :, :, cols].astype(jnp.float32).reshape(per, CHUNK).astype(jnp.bfloat16)
-            )
         ag_ref[...] = jnp.zeros_like(ag_ref)
         au_ref[...] = jnp.zeros_like(au_ref)
-
-        @pl.loop(0, nk)
-        def _(i, p=p):
-            xk = x2_ref[:, pl.ds(pl.multiple_of(i * CHUNK, CHUNK), CHUNK)]
-            gate_copy(p, i).wait()
-            ag_ref[...] += jnp.dot(xk, wg_ref[i], preferred_element_type=jnp.float32)
-            if p + 1 < pieces:
-                gate_copy(p + 1, i).start()
-            up_copy(p, i).wait()
-            au_ref[...] += jnp.dot(xk, wu_ref[i], preferred_element_type=jnp.float32)
-            if p + 1 < pieces:
-                up_copy(p + 1, i).start()
+        for g, group in enumerate(out_groups[p]):
+            drain(arr_ref.at[p, :, :, columns(group)], drecv_sem.at[p, g])
+            for j in range(*group):
+                cols = pl.ds(j * CHUNK, CHUNK)
+                x2_ref[:, cols] = (
+                    arr_ref[p, :, :, cols].astype(jnp.float32).reshape(per, CHUNK).astype(jnp.bfloat16)
+                )
+
+            @pl.loop(*group)
+            def _(i, p=p):
+                xk = x2_ref[:, pl.ds(pl.multiple_of(i * CHUNK, CHUNK), CHUNK)]
+                gate_copy(p, i).wait()
+                ag_ref[...] += jnp.dot(xk, wg_ref[i], preferred_element_type=jnp.float32)
+                if p + 1 < pieces:
+                    gate_copy(p + 1, i).start()
+                up_copy(p, i).wait()
+                au_ref[...] += jnp.dot(xk, wu_ref[i], preferred_element_type=jnp.float32)
+                if p + 1 < pieces:
+                    up_copy(p + 1, i).start()
 
         g = ag_ref[...]
         inner_ref[...] = (g / (1.0 + jnp.exp(-g)) * au_ref[...]).astype(jnp.bfloat16)
@@ -252,15 +255,14 @@
 
     o_copy.wait()
     for p in range(pieces):
-        drain(send_ref.at[p], dsend_sem.at[p])
+        for g, group in enumerate(out_groups[p]):
+            drain(send_ref.at[p, :, :, columns(group)], dsend_sem.at[p, g])
         for g, group in enumerate(groups[p]):
             drain(yb_ref.at[p, :, :, columns(group)], rsend_sem.at[p, g])
-
 
 def hand_over(latent_ref, moe_ref, latent_out_ref, moe_out_ref):
     latent_out_ref[...] = latent_ref[...]
     moe_out_ref[...] = moe_ref[...]
-
 
 def shards(
     queries,
@@ -323,10 +325,10 @@
             dma((nk,)),
             dma((nk,)),
             dma((nk,)),
-            dma((pieces,)),
-            dma((pieces,)),
-            dma((pieces, 2)),
-            dma((pieces, 2)),
+            dma((pieces, 3)),
+            dma((pieces, 3)),
+            dma((pieces, 3)),
+            dma((pieces, 3)),
         ],
         compiler_params=pltpu.CompilerParams(
             collective_id=0, has_side_effects=True, vmem_limit_bytes=60 * 1024 * 1024
@@ -358,7 +360,6 @@
         out_specs=(vmem, vmem),
     )(latent_out, moe_out)
 
-
 def solution(mesh):
     return jax.shard_map(
         shards,

time: 45.1 us -> 41.6 us (0.922)
  Pallas kernels: 44.3 us -> 40.7 us
    pallas_call x1, Pallas kernels: 42.5 us -> 39 us  [shards(): pl.pallas_call(functools.partial(kernel, n, n_member, pieces, cap, expert...]
where the time goes in v3:
time: 41.6 us; the launch traced here: 41.4 us
  Pallas kernels  40.7 us (98%)
  between operations  0.64 us (2%)
    pallas_call x1, Pallas kernels, shards(): pl.pallas_call(functools.partial(kernel, n, n_member, pieces, cap, expert...  39 us
    pallas_call x1, Pallas kernels, shards(): pl.pallas_call(hand_over, out_shape=(jax.ShapeDtypeStruct(latent_out.shap...  1.78 us

profile of v3, /device:TPU:0, one launch (start us, length us, event | category | flops | bytes accessed | tf_op | source)
XLA Modules:
  0.0 41.4 jit_solution(218341075791169352)
XLA Ops:
  0.6 39.0 %shard_map.113 = (bf16[6,64,512]{2,1,0:T(8,128)(2,1)}, bf16[6,3584]{1,0:T(8,128)(2,1)}) custom-call(s32[32]{0:T(128)} %placement_ref.1, s32[6]{0:T(128)} %lengths_ref.1, s32[6,8]{1,0:T(8,128)} %ids_ref.1, f32[6,8]{1,0:T(8,128)} %scores_ref.1, bf16[6,3584]{1,0:T(8,128)(2,1)} %x_ref.1, bf16[6,64,576]{2,1,0:T(8,128)(2,1)} %q_hbm.1, ...), custom_call_target="tpu_custom_call" | custom-call | flops 2818572288 | bytes 88080384 | tf_op jit(solution)/shard_map/pallas_call | solution.py:296
  39.6 1.8 %shard_map.114 = (bf16[6,64,512]{2,1,0:T(8,128)(2,1)}, bf16[6,3584]{1,0:T(8,128)(2,1)}) custom-call(bf16[6,64,512]{2,1,0:T(8,128)(2,1)} %get-tuple-element.4.latent_ref, bf16[6,3584]{1,0:T(8,128)(2,1)} %get-tuple-element.5.moe_ref), custom_call_target="tpu_custom_call" | custom-call | tf_op jit(solution)/shard_map/pallas_call | solution.py:353

commit v4 on v3

--- a/solution.py
+++ b/solution.py
@@ -133,9 +133,9 @@
             )
             send_ref[p, :, :, cols] = made.reshape(n, cap, CHUNK).astype(jnp.bfloat16)
 
-    cut, far = nk * 2 // 7, nk * 4 // 7
-
-    out_groups = [[(0, cut), (cut, far), (far, nk)]] + [[(0, nk)]] * (pieces - 1)
+    first, cut, far = nk // 7, nk * 2 // 7, nk * 4 // 7
+
+    out_groups = [[(0, first), (first, cut), (cut, far), (far, nk)]] + [[(0, nk)]] * (pieces - 1)
     groups = [[(0, nk)]] * (pieces - 1) + [[(0, far), (far, nk)]]
 
     def columns(group):
@@ -325,10 +325,10 @@
             dma((nk,)),
             dma((nk,)),
             dma((nk,)),
-            dma((pieces, 3)),
-            dma((pieces, 3)),
-            dma((pieces, 3)),
-            dma((pieces, 3)),
+            dma((pieces, 4)),
+            dma((pieces, 4)),
+            dma((pieces, 4)),
+            dma((pieces, 4)),
         ],
         compiler_params=pltpu.CompilerParams(
             collective_id=0, has_side_effects=True, vmem_limit_bytes=60 * 1024 * 1024

time: 41.6 us -> 41.6 us (level)
  no operation moved by 1% of the time
where the time goes in v4:
time: 41.6 us; the launch traced here: 41.4 us
  Pallas kernels  40.8 us (98%)
  between operations  0.64 us (2%)
    pallas_call x1, Pallas kernels, shards(): pl.pallas_call(functools.partial(kernel, n, n_member, pieces, cap, expert...  39 us
    pallas_call x1, Pallas kernels, shards(): pl.pallas_call(hand_over, out_shape=(jax.ShapeDtypeStruct(latent_out.shap...  1.78 us

profile of v4, /device:TPU:0, one launch (start us, length us, event | category | flops | bytes accessed | tf_op | source)
XLA Modules:
  0.0 41.4 jit_solution(11397208741157475284)
XLA Ops:
  0.6 39.0 %shard_map.113 = (bf16[6,64,512]{2,1,0:T(8,128)(2,1)}, bf16[6,3584]{1,0:T(8,128)(2,1)}) custom-call(s32[32]{0:T(128)} %placement_ref.1, s32[6]{0:T(128)} %lengths_ref.1, s32[6,8]{1,0:T(8,128)} %ids_ref.1, f32[6,8]{1,0:T(8,128)} %scores_ref.1, bf16[6,3584]{1,0:T(8,128)(2,1)} %x_ref.1, bf16[6,64,576]{2,1,0:T(8,128)(2,1)} %q_hbm.1, ...), custom_call_target="tpu_custom_call" | custom-call | flops 2818572288 | bytes 88080384 | tf_op jit(solution)/shard_map/pallas_call | solution.py:296
  39.7 1.8 %shard_map.114 = (bf16[6,64,512]{2,1,0:T(8,128)(2,1)}, bf16[6,3584]{1,0:T(8,128)(2,1)}) custom-call(bf16[6,64,512]{2,1,0:T(8,128)(2,1)} %get-tuple-element.4.latent_ref, bf16[6,3584]{1,0:T(8,128)(2,1)} %get-tuple-element.5.moe_ref), custom_call_target="tpu_custom_call" | custom-call | tf_op jit(solution)/shard_map/pallas_call | solution.py:353
